TPU v7x, 32 devices: a whole 2x2x4 slice. The times are simulated.
32 devices in a mesh: dp: 8 (over y, x, core), expert: 4 (over z).
Axes of the slice: x: 2, y: 2, z: 4, core: 2. Of those that a mesh axis runs over, the one named last changes fastest.
Arguments:
- tokens: bfloat16 [4096, 2560], P(('dp', 'expert')), may hold values from -6 to 6
- cotangent: bfloat16 [4096, 2560], P(('dp', 'expert')), may hold values from -6 to 6
- routes: int32 [4096, 6], P(('dp', 'expert')), may hold values from 0 to 159, all different within a row
- gates: float32 [4096, 6], P(('dp', 'expert')), may hold values from 0.05 to 0.5
- layout: int32 [3, 4], replicated, may hold values from 0 to 3, as said below
- weights: bfloat16 [4, 2560, 768], P('expert', 'dp'), may hold values from -0.125 to 0.125
- first_moment: float32 [4, 2560, 768], P('expert', 'dp'), may hold values from -12 to 12
- second_moment: float32 [4, 2560, 768], P('expert', 'dp'), may hold values from 0.5 to 50
Outputs:
- grad_input: bfloat16 [4096, 2560], P(('dp', 'expert'))
- new_first: float32 [4, 2560, 768], P('expert', 'dp')
- new_second: float32 [4, 2560, 768], P('expert', 'dp')
Inputs may be any that keep to these rules, and one draw needn't show every extreme that they name: `routes`: each token names 6 different experts. Row 0 is a permutation of the slots; row 1 is i XOR m for one m of 1 to 3, the same for every i, so that i and layout[1, i] form a pair; row 2 holds 0 or 1, equal for both members of a pair; some pair swaps and, where there are two pairs or more, some pair keeps its slots.
All inputs are finite; a program needn't handle non-finite values.
Results may differ from a plain program's by a relative error of at most 0.015.
Values may be sent and summed in bfloat16 or wider, within the bound.
No kernel may reach another device: no remote copies, remote signals or barrier semaphores. Data moves between devices by JAX's collectives and lax.ppermute only.
A program may use at most 64 MiB of HBM per device.

v0:
```python
import jax
import jax.numpy as jnp
from jax import lax
from jax.sharding import Mesh, PartitionSpec as P

HSPLIT = 4
CAP = 8


first_decay = 0.9
second_decay = 0.999

DP = ("outer", "inner", "core")
CHIPS = ("outer", "inner")
ROWS = DP + ("expert",)


def xor_rounds(block, xor_mask):
    count = lax.axis_size("expert")
    for bit_pos in range(count.bit_length() - 1):
        route = [(lane, lane ^ (1 << bit_pos)) for lane in range(count)]
        partner_copy = lax.ppermute(block, "expert", route)
        flip_now = jnp.bitwise_and(jnp.right_shift(xor_mask, bit_pos), 1) == 1
        block = jnp.where(flip_now, partner_copy, block)
    return block


def select_lane(values, lane_ids, index_now):
    return jnp.sum(jnp.where(lane_ids == index_now, values, 0))


def exchange(block, axes):
    return lax.all_to_all(block, axes, split_axis=0, concat_axis=0, tiled=True)


def body(move, active, tokens, cotangent, routes, gates, expert_at, weights, first_moment, second_moment):
    n_expert = lax.axis_size("expert")
    n_chip = lax.axis_size(CHIPS)
    n_window = n_expert // HSPLIT
    tok_dev, top_count = routes.shape
    width = tokens.shape[1]
    own_depth = weights.shape[1]
    depth = 2 * own_depth
    width_dev = weights.shape[2] // 3
    bf16 = jnp.bfloat16
    core = lax.axis_index("core")

    block = weights[0]
    if n_window > 1:
        block = jnp.where(active, move(block), block)
    chip_weights = lax.all_gather(block, "core", axis=0, tiled=True)

    flat_ids = routes.reshape(-1)
    window_ids = jnp.arange(n_window, dtype=jnp.int32)
    hit_table = (flat_ids[:, None] == window_ids[None, :]).astype(jnp.int32)
    earlier = jnp.cumsum(hit_table, axis=0) - hit_table
    position = jnp.sum(earlier * hit_table, axis=1)
    kept = (flat_ids < n_window) & (position < CAP)
    slot_key = jnp.where(kept, flat_ids * CAP + position, -1)
    slot_pick = (jnp.arange(n_window * CAP, dtype=jnp.int32)[:, None] == slot_key[None, :]).astype(
        jnp.float32
    )
    assign_pick = slot_pick.reshape(n_window * CAP, tok_dev, top_count)
    slot_token = jnp.sum(assign_pick, axis=2)
    slot_gate = jnp.sum(assign_pick * gates[None], axis=(1, 2))[:, None]
    rows = jnp.dot(slot_token.astype(bf16), tokens, preferred_element_type=jnp.float32).astype(bf16)
    grads = jnp.dot(slot_token.astype(bf16), cotangent, preferred_element_type=jnp.float32)
    grads = (grads * slot_gate).astype(bf16)
    sends = jnp.stack((rows, grads)).reshape(2, n_window, CAP, n_chip, depth).transpose(3, 1, 0, 2, 4)
    if n_window == 1:
        sends = jnp.broadcast_to(sends, (n_chip, n_expert, 2, CAP, depth))
        dest_token = jnp.broadcast_to(slot_token[None], (n_expert, CAP, tok_dev))
    else:
        sends = jnp.take(sends, expert_at, axis=1)
        dest_token = jnp.take(slot_token.reshape(n_window, CAP, tok_dev), expert_at, axis=0)
    dest_token = dest_token.reshape(n_expert * CAP, tok_dev).astype(bf16)
    got = exchange(sends.reshape(n_chip * n_expert, 2, CAP, depth), CHIPS + ("expert",))
    rows_in = got[:, 0].reshape(-1, depth)
    grads_in = got[:, 1].reshape(-1, depth)

    pre_part = jnp.dot(rows_in, chip_weights[:, : 2 * width_dev], preferred_element_type=jnp.float32)
    grad_part = jnp.dot(grads_in, chip_weights[:, 2 * width_dev :], preferred_element_type=jnp.float32)
    parts = jnp.concatenate((pre_part, grad_part), axis=1).astype(bf16)
    if n_chip > 4:
        sums = exchange(parts.reshape(n_chip, -1, parts.shape[1]), CHIPS)
        sums = jnp.sum(sums.astype(jnp.float32), axis=0).astype(bf16)
        sums = lax.all_gather(sums, CHIPS, axis=0, tiled=True).astype(jnp.float32)
    else:
        sums = jnp.sum(lax.all_gather(parts, CHIPS, axis=0).astype(jnp.float32), axis=0)
    gate_pre = sums[:, :width_dev]
    up_pre = sums[:, width_dev : 2 * width_dev]
    hidden_grad = sums[:, 2 * width_dev :]
    sigma = jax.nn.sigmoid(gate_pre)
    active_part = gate_pre * sigma
    hidden = active_part * up_pre
    gate_grad = hidden_grad * up_pre * sigma * (1.0 + gate_pre * (1.0 - sigma))
    up_grad = hidden_grad * active_part
    acts = jnp.concatenate((gate_grad, up_grad, hidden), axis=1).astype(bf16)
    part_rows = lax.dot_general(
        acts[:, : 2 * width_dev],
        chip_weights[:, : 2 * width_dev],
        (((1,), (1,)), ((), ())),
        preferred_element_type=jnp.float32,
    ).astype(bf16)
    returned = exchange(part_rows.reshape(n_chip * n_expert, CAP, depth), CHIPS + ("expert",))
    returned = returned.reshape(n_chip, n_expert * CAP, depth).transpose(1, 0, 2).reshape(-1, width)
    grad_input = lax.dot_general(
        dest_token, returned, (((0,), (0,)), ((), ())), preferred_element_type=jnp.float32
    ).astype(bf16)

    if n_window == 1:
        acts = jnp.where(active, move(acts), acts)
    proj_grad = lax.dot_general(
        rows_in, acts[:, : 2 * width_dev], (((0,), (0,)), ((), ())), preferred_element_type=jnp.float32
    )
    down_grad = lax.dot_general(
        grads_in, acts[:, 2 * width_dev :], (((0,), (0,)), ((), ())), preferred_element_type=jnp.float32
    )
    weight_grad = jnp.concatenate((proj_grad, down_grad), axis=1)
    low, high = weight_grad[:own_depth], weight_grad[own_depth:]
    other = lax.ppermute(jnp.where(core == 0, high, low).astype(bf16), "core", [(0, 1), (1, 0)])
    weight_grad = jnp.where(core == 0, low, high) + other.astype(jnp.float32)
    moments = jnp.stack((first_moment[0], second_moment[0]))
    moved = move(moments.astype(bf16)).astype(jnp.float32)
    moments = jnp.where(active, moved, moments)
    new_first = first_decay * moments[0] + (1.0 - first_decay) * weight_grad
    new_second = second_decay * moments[1] + (1.0 - second_decay) * weight_grad * weight_grad
    return grad_input, new_first[None], new_second[None]


def local(tokens, cotangent, routes, gates, layout, weights, first_moment, second_moment):
    n_expert = lax.axis_size("expert")
    own_index = lax.axis_index("expert")
    args = (tokens, cotangent, routes, gates)
    rest = (weights, first_moment, second_moment)
    swap_on = layout[2]
    if n_expert != 4:
        lane_ids = jnp.arange(n_expert, dtype=jnp.int32)
        placement = layout[0]
        xor_mask = layout[1, 0]
        held_slot = jnp.where(swap_on == 1, jnp.bitwise_xor(lane_ids, xor_mask), lane_ids)
        inverse = jnp.sum(
            jnp.where(placement[None, :] == lane_ids[:, None], lane_ids[None, :], 0), axis=1
        )
        slot_owner = inverse // HSPLIT
        expert_at = jnp.sum(
            jnp.where(held_slot[:, None] == lane_ids[None, :], slot_owner[None, :], 0), axis=1
        )
        active = select_lane(swap_on, lane_ids, own_index) == 1
        return body(lambda block: xor_rounds(block, xor_mask), active, *args, expert_at, *rest)
    pairs = [(low, high) for low in range(4) for high in range(low + 1, 4)]

    def branch(pair):
        low, high = pair

        def run(*operands):
            active = (own_index == low) | (own_index == high)
            move = lambda block: lax.ppermute(block, "expert", [(low, high), (high, low)])
            return body(move, active, *operands[:4], None, *operands[4:])

        return run

    case = jnp.sum(swap_on * jnp.array([-1, 1, 2, 3], dtype=jnp.int32))
    return lax.switch(case, [branch(pair) for pair in pairs], *args, *rest)


def solution(mesh):
    n_dp, n_expert = mesh.devices.shape
    split = Mesh(mesh.devices.reshape(n_dp // 4, 2, 2, n_expert), ROWS)
    in_specs = (
        P(ROWS, None),
        P(ROWS, None),
        P(ROWS, None),
        P(ROWS, None),
        P(),
        P("expert", DP, None),
        P("expert", DP, None),
        P("expert", DP, None),
    )
    out_specs = (P(ROWS, None), P("expert", DP, None), P("expert", DP, None))
    return jax.shard_map(local, mesh=split, in_specs=in_specs, out_specs=out_specs, check_vma=False)
```

profile of v0, /device:TPU:0, one launch (start us, length us, event | category | flops | bytes accessed | tf_op | source)
XLA Modules:
  0.0 81.7 jit_solution(14982146101792864048)
XLA Ops:
  0.6 1.3 %multiply_reduce_fusion = s32[]{:T(128)} fusion(s32[1,4]{1,0:T(1,128)} %constant.211, s32[3,4]{1,0:T(4,128)} %param.19), kind=kLoop, calls=%fused_computation.372 | loop fusion | flops 7 | bytes 36 | tf_op jit(solution)/shard_map/reduce_sum | solution.py:163
  2.6 79.1 %conditional.2 = (bf16[128,2560]{1,0:T(8,128)(2,1)}, f32[1,320,768]{2,1,0:T(8,128)}, f32[1,320,768]{2,1,0:T(8,128)}) conditional(s32[]{:T(128)} %clamp.3, (s32[128,6]{0,1:T(8,128)}, bf16[128,2560]{1,0:T(8,128)(2,1)}, bf16[128,2560]{1,0:T(8,128)(2,1)}, f32[128,6]{0,1:T(8,128)}, bf16[1,320,768]{2,1,0:T(8,128)(2,1)}, ...), branch_computations={%region_1.7_spmd, %region_7.13_spmd, %region_13.0_spmd, %region_19... | conditional | flops 377169952 | bytes 85958432
  2.8 0.0 copy-start.4
  2.9 0.9 %copy.272 = s32[128,6]{1,0:T(8,128)S(1)} copy(s32[128,6]{0,1:T(8,128)} %get-tuple-element.444) | data formatting | bytes 6144 | tf_op jit(solution)/shard_map
  3.7 0.1 reshape.946
  3.9 0.3 reduce-window.40
  4.2 0.1 reshape.926
  4.3 0.2 slice_reduce_fusion.4
  4.5 0.2 reduce-window.41
  4.7 0.1 broadcast.522
  4.8 0.1 reshape.929
  4.9 0.1 copy.258
  5.0 0.8 %select_reduce_fusion.4 = (f32[8]{0:T(128)S(1)}, bf16[8,128]{1,0:T(8,128)(2,1)S(1)}) fusion(f32[128,6]{0,1:T(8,128)} %get-tuple-element.135, s32[128,6]{0,1:T(8,128)S(1)} %copy.258), kind=kLoop, calls=%fused_computation.299 | loop fusion | flops 29688 | bytes 8224 | tf_op jit(solution)/shard_map/cond/branch_4_fun/reduce_sum | solution.py:65
  5.8 1.3 %convolution_convert_fusion.16 = bf16[8,2560]{1,0:T(8,128)(2,1)S(1)} fusion(bf16[8,128]{1,0:T(8,128)(2,1)S(1)} %get-tuple-element.469, bf16[128,2560]{1,0:T(8,128)(2,1)} %get-tuple-element.133), kind=kOutput, calls=%fused_computation.250 | convolution fusion | flops 5263360 | bytes 698368 | tf_op jit(solution)/shard_map/cond/branch_4_fun/dot_general | solution.py:66
  7.1 0.0 copy-start.16
  7.1 1.3 %fusion.108 = bf16[8,2560]{1,0:T(8,128)(2,1)S(1)} fusion(bf16[8,128]{1,0:T(8,128)(2,1)S(1)} %get-tuple-element.469, bf16[128,2560]{1,0:T(8,128)(2,1)} %get-tuple-element.134, f32[8]{0:T(128)S(1)} %get-tuple-element.468), kind=kOutput, calls=%fused_computation.249 | convolution fusion | flops 5283840 | bytes 698400 | tf_op jit(solution)/shard_map/cond/branch_4_fun/dot_general | solution.py:67
  8.5 0.8 broadcast_in_dim.135
  9.2 8.3 %all-to-all-start.8 = ((bf16[16,2,8,640]{3,2,1,0:T(8,128)(2,1)}), bf16[16,2,8,640]{3,2,1,0:T(8,128)(2,1)S(1)}, u32[]{:S(2)}, u32[]{:S(2)}) async-start(bf16[16,2,8,640]{3,2,1,0:T(8,128)(2,1)} %bitcast.82), calls=%async_computation.8 | async-start | bytes 655360 | tf_op jit(solution)/shard_map/cond/branch_4_fun/all_to_all | solution.py:33
  17.6 0.0 copy-done.4
  17.6 1.0 %constant_dynamic-update-slice_fusion.9 = f32[2,320,768]{2,1,0:T(8,128)} fusion(f32[1,320,768]{2,1,0:T(8,128)S(1)} %copy-done.4), kind=kLoop, calls=%fused_computation.305 | loop fusion | bytes 1966080 | tf_op jit(solution)/shard_map/conditional
  18.6 0.0 copy-done.16
  18.6 2.5 %all-gather.4 = bf16[1,640,768]{2,1,0:T(8,128)(2,1)S(1)} all-gather(bf16[1,320,768]{2,1,0:T(8,128)(2,1)S(1)} %copy-done.16), channel_id=6, replica_groups=mesh['outer'=2,'inner'=2,'core'=2,'expert'=4] {'core'}, dimensions={1}, use_global_device_ids=true | all-gather | bytes 1474560 | tf_op jit(solution)/shard_map/cond/branch_4_fun/all_gather | solution.py:51
  21.1 8.5 %all-to-all-done.8 = bf16[16,2,8,640]{3,2,1,0:T(8,128)(2,1)S(1)} async-done(((bf16[16,2,8,640]{3,2,1,0:T(8,128)(2,1)}), bf16[16,2,8,640]{3,2,1,0:T(8,128)(2,1)S(1)}, u32[]{:S(2)}, u32[]{:S(2)}) %all-to-all-start.8) | async-done | bytes 327712 | tf_op jit(solution)/shard_map/cond/branch_4_fun/all_to_all | solution.py:33
  29.5 0.0 copy-start.47
  29.5 0.2 fusion.111
  29.8 0.5 copy-done.47
  30.3 0.3 fusion.110
  30.5 0.0 copy-start.10
  30.5 0.0 copy-start.30
  30.6 10.7 %all_gather.39 = bf16[4,128,768]{2,1,0:T(8,128)(2,1)S(1)} all-gather(bf16[1,128,768]{2,1,0:T(8,128)(2,1)S(1)} %pad_maximum_fusion.13), channel_id=1, replica_groups=mesh['outer'=2,'inner'=2,'core'=2,'expert'=4] {'outer','inner'}, dimensions={0}, use_global_device_ids=true | all-gather | bytes 983040 | tf_op jit(solution)/shard_map/cond/branch_4_fun/all_gather | solution.py:89
  41.3 0.1 convert_reduce_fusion.8
  41.4 0.1 multiply_convert_fusion.12
  41.5 0.7 collective-permute-start.13
  42.2 0.0 copy-done.10
  42.2 0.0 copy-done.30
  42.2 0.1 constant_dynamic-update-slice_fusion.8
  42.3 0.0 copy-start.31
  42.3 1.3 %copy-done.31 = f32[2,320,768]{2,1,0:T(8,128)} copy-done((f32[2,320,768]{2,1,0:T(8,128)}, f32[2,320,768]{2,1,0:T(8,128)S(1)}, u32[]{:S(2)}) %copy-start.31) | copy-done | bytes 1966104 | tf_op jit(solution)/shard_map/conditional
  43.6 0.0 copy-start.48
  43.6 1.0 %convert_element_type.404 = bf16[2,320,768]{2,1,0:T(8,128)(2,1)} convert(f32[2,320,768]{2,1,0:T(8,128)S(1)} %constant_dynamic-update-slice_fusion.8) | non-fusion elementwise | flops 491520 | bytes 2949120 | tf_op jit(solution)/shard_map/cond/branch_4_fun/convert_element_type | solution.py:124
  44.6 1.6 %collective-permute-start.12 = (bf16[2,320,768]{2,1,0:T(8,128)(2,1)}, bf16[2,320,768]{2,1,0:T(8,128)(2,1)}, u32[]{:S(2)}, u32[]{:S(2)}) collective-permute-start(bf16[2,320,768]{2,1,0:T(8,128)(2,1)} %convert_element_type.404), channel_id=1, source_target_pairs={{1,3},{3,1},{5,7},{7,5},{9,11},{11,9},{13,15},{15,13},{17,19},{19,... | collective-permute-start | bytes 2949128 | tf_op jit(solution)/shard_map/cond/branch_4_fun/ppermute | solution.py:158
  46.3 1.0 %fusion.109 = bf16[16,8,640]{2,1,0:T(8,128)(2,1)} fusion(bf16[640,768]{1,0:T(8,128)(2,1)S(1)} %bitcast.329, bf16[128,256]{1,0:T(8,128)(2,1)S(1)} %get-tuple-element.498, bf16[128,256]{1,0:T(8,128)(2,1)S(1)} %get-tuple-element.497), kind=kOutput, calls=%fused_computation.258 | convolution fusion | flops 84230144 | bytes 950272 | tf_op jit(solution)/shard_map/cond/branch_4_fun/dot_general | solution.py:99
  47.3 7.5 %all-to-all-start.9 = ((bf16[16,8,640]{2,1,0:T(8,128)(2,1)}), bf16[16,8,640]{2,1,0:T(8,128)(2,1)S(1)}, u32[]{:S(2)}, u32[]{:S(2)}) async-start(bf16[16,8,640]{2,1,0:T(8,128)(2,1)} %fusion.109), calls=%async_computation.9 | async-start | bytes 327680 | tf_op jit(solution)/shard_map/cond/branch_4_fun/all_to_all | solution.py:33
  54.7 0.0 collective-permute-done.13
  54.7 0.1 broadcast_select_fusion.4
  54.8 0.0 copy-done.48
  54.8 0.4 fusion.122
  55.2 0.3 fusion.123
  55.4 0.0 copy-start.41
  55.5 0.8 %copy-done.41 = f32[640,256]{1,0:T(8,128)} copy-done((f32[640,256]{1,0:T(8,128)}, f32[640,256]{1,0:T(8,128)S(1)}, u32[]{:S(2)}) %copy-start.41) | copy-done | bytes 655384 | tf_op jit(solution)/shard_map/conditional
  56.3 0.0 copy-start.32
  56.3 0.9 %select_convert_fusion.4 = bf16[320,768]{1,0:T(8,128)(2,1)} fusion(pred[]{:T(512)S(6)} %eq.250, f32[640,256]{1,0:T(8,128)S(1)} %fusion.123, f32[640,512]{1,0:T(8,128)S(1)} %fusion.122), kind=kLoop, calls=%fused_computation.273 | loop fusion | flops 2211840 | bytes 2457601 | tf_op jit(solution)/shard_map/cond/branch_4_fun/convert_element_type | solution.py:121
  57.2 0.0 collective-permute-start.14
  57.2 18.4 %all-to-all-done.9 = bf16[16,8,640]{2,1,0:T(8,128)(2,1)S(1)} async-done(((bf16[16,8,640]{2,1,0:T(8,128)(2,1)}), bf16[16,8,640]{2,1,0:T(8,128)(2,1)S(1)}, u32[]{:S(2)}, u32[]{:S(2)}) %all-to-all-start.9) | async-done | bytes 163872 | tf_op jit(solution)/shard_map/cond/branch_4_fun/all_to_all | solution.py:33
  75.6 1.2 %fusion.131 = bf16[128,2560]{1,0:T(8,128)(2,1)} fusion(bf16[32,2560]{1,0:T(8,128)(2,1)S(1)} %bitcast.352, bf16[8,128]{1,0:T(8,128)(2,1)S(1)} %get-tuple-element.469), kind=kOutput, calls=%fused_computation.302 | convolution fusion | flops 20971520 | bytes 821248 | tf_op jit(solution)/shard_map/cond/branch_4_fun/dot_general | solution.py:107
  76.8 0.0 copy-start.42
  76.8 0.0 collective-permute-done.12
  76.8 0.0 copy-done.32
  76.8 1.5 %convert_select_fusion.4 = f32[2,320,768]{2,1,0:T(8,128)S(1)} fusion(f32[2,320,768]{2,1,0:T(8,128)S(1)} %copy-done.32, bf16[2,320,768]{2,1,0:T(8,128)(2,1)} %collective-permute-done.12, pred[]{:T(512)S(6)} %or.16), kind=kLoop, calls=%fused_computation.253 | loop fusion | flops 983040 | bytes 4915201 | tf_op jit(solution)/shard_map/cond/branch_4_fun/jit(_where)/select_n | solution.py:125
  78.3 0.0 collective-permute-done.14
  78.3 0.0 copy-done.42
  78.3 2.3 %fusion.113 = (f32[1,320,768]{2,1,0:T(8,128)}, f32[320,768]{1,0:T(8,128)S(1)}) fusion(f32[2,320,768]{2,1,0:T(8,128)S(1)} %convert_select_fusion.4, bf16[320,768]{1,0:T(8,128)(2,1)} %collective-permute-done.14, f32[640,256]{1,0:T(8,128)S(1)} %copy-done.42, f32[640,512]{1,0:T(8,128)S(1)} %fusion.122, pred[]{:T(512)S(6)} %eq.250), kind=kLoop, calls=%fused_computation.263 | loop fusion | flops 2211840 | bytes 5406721 | tf_op jit(solution)/shard_map/cond/branch_4_fun/broadcast_in_dim | solution.py:128
  80.6 1.1 %fusion.118 = f32[1,320,768]{2,1,0:T(8,128)} fusion(f32[2,320,768]{2,1,0:T(8,128)S(1)} %convert_select_fusion.4, f32[320,768]{1,0:T(8,128)S(1)} %get-tuple-element.481), kind=kLoop, calls=%fused_computation.271 | loop fusion | flops 737280 | bytes 2949120 | tf_op jit(solution)/shard_map/cond/branch_4_fun/broadcast_in_dim | solution.py:128
  (8 shorter events, 0.1 us)
Async XLA Ops:
  2.8 14.7 %copy-start.4 = (f32[1,320,768]{2,1,0:T(8,128)S(1)}, f32[1,320,768]{2,1,0:T(8,128)}, u32[]{:S(2)}) copy-start(f32[1,320,768]{2,1,0:T(8,128)} %get-tuple-element.138) | copy-start | bytes 2949124 | tf_op jit(solution)/shard_map/conditional
  7.1 11.5 %copy-start.16 = (bf16[1,320,768]{2,1,0:T(8,128)(2,1)S(1)}, bf16[1,320,768]{2,1,0:T(8,128)(2,1)}, u32[]{:S(2)}) copy-start(bf16[1,320,768]{2,1,0:T(8,128)(2,1)} %get-tuple-element.136) | copy-start | bytes 1474564 | tf_op jit(solution)/shard_map/conditional
  9.2 20.3 %all-to-all-start.8 = ((bf16[16,2,8,640]{3,2,1,0:T(8,128)(2,1)}), bf16[16,2,8,640]{3,2,1,0:T(8,128)(2,1)S(1)}, u32[]{:S(2)}, u32[]{:S(2)}) async-start(bf16[16,2,8,640]{3,2,1,0:T(8,128)(2,1)} %bitcast.82), calls=%async_computation.8 | async-start | bytes 655360 | tf_op jit(solution)/shard_map/cond/branch_4_fun/all_to_all | solution.py:33
  29.5 0.7 copy-start.47
  30.5 11.7 %copy-start.10 = (f32[1,320,768]{2,1,0:T(8,128)S(1)}, f32[1,320,768]{2,1,0:T(8,128)}, u32[]{:S(2)}) copy-start(f32[1,320,768]{2,1,0:T(8,128)} %get-tuple-element.139) | copy-start | bytes 2949124 | tf_op jit(solution)/shard_map/conditional
  30.5 11.7 %copy-start.30 = (f32[2,320,768]{2,1,0:T(8,128)S(1)}, f32[2,320,768]{2,1,0:T(8,128)}, u32[]{:S(2)}) copy-start(f32[2,320,768]{2,1,0:T(8,128)} %constant_dynamic-update-slice_fusion.9) | copy-start | bytes 5898244 | tf_op jit(solution)/shard_map/conditional
  41.5 13.2 %collective-permute-start.13 = (bf16[128,768]{1,0:T(8,128)(2,1)S(1)}, bf16[128,768]{1,0:T(8,128)(2,1)S(1)}, u32[]{:S(2)}, u32[]{:S(2)}) collective-permute-start(bf16[128,768]{1,0:T(8,128)(2,1)S(1)} %pad_maximum_fusion.14), channel_id=1, source_target_pairs={{1,3},{3,1},{5,7},{7,5},{9,11},{11,9},{13,15},{15,13},{17,19},{19,... | collective-permute-start | bytes 589832 | tf_op jit(solution)/shard_map/cond/branch_4_fun/ppermute | solution.py:158
  42.3 1.3 %copy-start.31 = (f32[2,320,768]{2,1,0:T(8,128)}, f32[2,320,768]{2,1,0:T(8,128)S(1)}, u32[]{:S(2)}) copy-start(f32[2,320,768]{2,1,0:T(8,128)S(1)} %constant_dynamic-update-slice_fusion.8) | copy-start | bytes 5898244 | tf_op jit(solution)/shard_map/conditional
  43.6 11.2 %copy-start.48 = (bf16[16,2,8,640]{3,2,1,0:T(8,128)(2,1)S(1)}, bf16[16,2,8,640]{3,2,1,0:T(8,128)(2,1)}, u32[]{:S(2)}) copy-start(bf16[16,2,8,640]{3,2,1,0:T(8,128)(2,1)} %copy-done.47) | copy-start | bytes 983044 | tf_op jit(solution)/shard_map/conditional
  44.6 32.2 %collective-permute-start.12 = (bf16[2,320,768]{2,1,0:T(8,128)(2,1)}, bf16[2,320,768]{2,1,0:T(8,128)(2,1)}, u32[]{:S(2)}, u32[]{:S(2)}) collective-permute-start(bf16[2,320,768]{2,1,0:T(8,128)(2,1)} %convert_element_type.404), channel_id=1, source_target_pairs={{1,3},{3,1},{5,7},{7,5},{9,11},{11,9},{13,15},{15,13},{17,19},{19,... | collective-permute-start | bytes 2949128 | tf_op jit(solution)/shard_map/cond/branch_4_fun/ppermute | solution.py:158
  47.3 28.3 %all-to-all-start.9 = ((bf16[16,8,640]{2,1,0:T(8,128)(2,1)}), bf16[16,8,640]{2,1,0:T(8,128)(2,1)S(1)}, u32[]{:S(2)}, u32[]{:S(2)}) async-start(bf16[16,8,640]{2,1,0:T(8,128)(2,1)} %fusion.109), calls=%async_computation.9 | async-start | bytes 327680 | tf_op jit(solution)/shard_map/cond/branch_4_fun/all_to_all | solution.py:33
  55.4 0.8 %copy-start.41 = (f32[640,256]{1,0:T(8,128)}, f32[640,256]{1,0:T(8,128)S(1)}, u32[]{:S(2)}) copy-start(f32[640,256]{1,0:T(8,128)S(1)} %fusion.123) | copy-start | bytes 1966084 | tf_op jit(solution)/shard_map/conditional
  56.3 20.5 %copy-start.32 = (f32[2,320,768]{2,1,0:T(8,128)S(1)}, f32[2,320,768]{2,1,0:T(8,128)}, u32[]{:S(2)}) copy-start(f32[2,320,768]{2,1,0:T(8,128)} %copy-done.31) | copy-start | bytes 5898244 | tf_op jit(solution)/shard_map/conditional
  57.2 21.1 %collective-permute-start.14 = (bf16[320,768]{1,0:T(8,128)(2,1)}, bf16[320,768]{1,0:T(8,128)(2,1)}, u32[]{:S(2)}, u32[]{:S(2)}) collective-permute-start(bf16[320,768]{1,0:T(8,128)(2,1)} %select_convert_fusion.4), channel_id=1, source_target_pairs={{0,4},{4,0},{1,5},{5,1},{2,6},{6,2},{3,7},{7,3},{8,12},{12,8},{9,1... | collective-permute-start | bytes 1474568 | tf_op jit(solution)/shard_map/cond/branch_4_fun/ppermute | solution.py:121
  76.8 1.5 %copy-start.42 = (f32[640,256]{1,0:T(8,128)S(1)}, f32[640,256]{1,0:T(8,128)}, u32[]{:S(2)}) copy-start(f32[640,256]{1,0:T(8,128)} %copy-done.41) | copy-start | bytes 1966084 | tf_op jit(solution)/shard_map/conditional
where the time goes:
time: 82.6 us; the launch traced here: 81.7 us
  waiting for transfers between devices  26.9 us (33%)
  starting transfers between devices  18.1 us (22%)
  blocking collectives  13.2 us (16%)
  other arithmetic  9.77 us (12%)
  local copies, waits for them, and re-layouts  6.11 us (7%)
  matrix products  5.91 us (7%)
  between operations  1.29 us (2%)
    all_to_all x2, waiting for transfers between devices, exchange(): return lax.all_to_all(block, axes, split_axis=0, concat_axis=0, tiled=True)  26.9 us
    all_to_all x2, starting transfers between devices, exchange(): return lax.all_to_all(block, axes, split_axis=0, concat_axis=0, tiled=True)  15.8 us
    all_gather x1, blocking collectives, body(): lax.all_gather(parts, CHIPS, axis=0).astype(jnp.float32)  10.7 us
    another operation x27, local copies, waits for them, and re-layouts  5.08 us
    broadcast_in_dim x2, other arithmetic, body(): return (grad_input, new_first[None], new_second[None])  3.39 us
    all_gather x1, blocking collectives, body(): chip_weights = lax.all_gather(block, 'core', axis=0, tiled=True)  2.5 us
    ppermute x2, starting transfers between devices, run(): lax.ppermute(block, 'expert', [(low, high), (high, low)])  2.3 us
  transfers between devices with their start and end apart: 5, of which 2 were waited for; matrix products, arithmetic and copies ran while one was open for 9% of the time, Pallas kernels for 0%

commit v1 on v0

v1 whole, which is shorter than its diff:
```python
import functools

import jax
import jax.numpy as jnp
from jax import lax
from jax.experimental import pallas as pl
from jax.experimental.pallas import tpu as pltpu
from jax.sharding import Mesh, PartitionSpec as P

HSPLIT = 4
CAP = 8


first_decay = 0.9
second_decay = 0.999

DP = ("outer", "inner", "core")
CHIPS = ("outer", "inner")
ROWS = DP + ("expert",)
ACROSS = CHIPS + ("expert",)
PAIRS = [(low, high) for low in range(4) for high in range(low + 1, 4)]
CUTS = (20, 30)


def xor_rounds(block, xor_mask):
    count = lax.axis_size("expert")
    for bit_pos in range(count.bit_length() - 1):
        route = [(lane, lane ^ (1 << bit_pos)) for lane in range(count)]
        partner_copy = lax.ppermute(block, "expert", route)
        flip_now = jnp.bitwise_and(jnp.right_shift(xor_mask, bit_pos), 1) == 1
        block = jnp.where(flip_now, partner_copy, block)
    return block


def select_lane(values, lane_ids, index_now):
    return jnp.sum(jnp.where(lane_ids == index_now, values, 0))


def exchange(block, axes):
    return lax.all_to_all(block, axes, split_axis=0, concat_axis=0, tiled=True)


def pick_kernel(layout_ref, routes_ref, gates_ref, tokens_ref, cot_ref, case_ref, sends_ref, pick_ref):
    n_chip, n_expert, _, depth = sends_ref.shape
    tok_dev = tokens_ref.shape[0]
    case_ref[0, 0] = layout_ref[2, 1] - layout_ref[2, 0] + 2 * layout_ref[2, 2] + 3 * layout_ref[2, 3]
    hit = jnp.where(routes_ref[...] == 0, 1.0, 0.0)
    gate = jnp.sum(hit * gates_ref[...], axis=0, keepdims=True)
    hit = jnp.broadcast_to(jnp.sum(hit, axis=0, keepdims=True), (CAP, tok_dev))
    row_ids = lax.broadcasted_iota(jnp.int32, (tok_dev, tok_dev), 0)
    col_ids = lax.broadcasted_iota(jnp.int32, (tok_dev, tok_dev), 1)
    before = jnp.where(row_ids < col_ids, 1.0, 0.0).astype(jnp.bfloat16)
    position = jnp.dot(hit.astype(jnp.bfloat16), before, preferred_element_type=jnp.float32)
    slots = lax.broadcasted_iota(jnp.int32, (CAP, tok_dev), 0).astype(jnp.float32)
    pick = jnp.where(position == slots, hit, 0.0)
    slot_gate = jnp.sum(pick * gate, axis=1, keepdims=True)
    pick = pick.astype(jnp.bfloat16)
    pick_ref[...] = pick
    for chip in range(n_chip):
        span = slice(chip * depth, (chip + 1) * depth)
        rows = jnp.dot(pick, tokens_ref[:, span], preferred_element_type=jnp.float32)
        grads = jnp.dot(pick, cot_ref[:, span], preferred_element_type=jnp.float32) * slot_gate
        both = jnp.concatenate((rows, grads), axis=0).astype(jnp.bfloat16)
        for expert in range(n_expert):
            sends_ref[chip, expert] = both


def pick_rows(layout, routes, gates, tokens, cotangent):
    tok_dev, width = tokens.shape
    n_chip, n_expert = lax.axis_size(CHIPS), lax.axis_size("expert")
    vmem = pl.BlockSpec(memory_space=pltpu.VMEM)
    smem = pl.BlockSpec(memory_space=pltpu.SMEM)
    return pl.pallas_call(
        pick_kernel,
        out_shape=(
            jax.ShapeDtypeStruct((1, 1), jnp.int32),
            jax.ShapeDtypeStruct((n_chip, n_expert, 2 * CAP, width // n_chip), jnp.bfloat16),
            jax.ShapeDtypeStruct((CAP, tok_dev), jnp.bfloat16),
        ),
        in_specs=[smem, vmem, vmem, vmem, vmem],
        out_specs=(smem, vmem, vmem),
        cost_estimate=pl.CostEstimate(
            flops=4 * CAP * tok_dev * width, bytes_accessed=8 * tok_dev * width, transcendentals=0
        ),
        name="pick_rows",
    )(layout, routes.T, gates.T, tokens, cotangent)


def update_kernel(flags_ref, first_ref, second_ref, moved_ref, grad_ref, other_ref, new_first_ref, new_second_ref):
    rows = first_ref.shape[0]
    active = flags_ref[0] == 1
    base = pl.multiple_of(flags_ref[1] * rows, 16)
    step = 16
    for low in range(0, rows, step):
        span = slice(low, low + step)
        grad = grad_ref[pl.ds(base + low, step)] + other_ref[span].astype(jnp.float32)
        moved = moved_ref[span].astype(jnp.float32)
        kept = jnp.where(active, moved, first_ref[span])
        new_first_ref[span] = first_decay * kept + (1.0 - first_decay) * grad
        moved = moved_ref[rows + low : rows + low + step].astype(jnp.float32)
        kept = jnp.where(active, moved, second_ref[span])
        new_second_ref[span] = second_decay * kept + (1.0 - second_decay) * grad * grad


def update(active, core, first, second, mid, grad, other):
    vmem = pl.BlockSpec(memory_space=pltpu.VMEM)
    smem = pl.BlockSpec(memory_space=pltpu.SMEM)
    flags = jnp.stack((active.astype(jnp.int32), core))
    return pl.pallas_call(
        update_kernel,
        out_shape=(jax.ShapeDtypeStruct(first.shape, jnp.float32),) * 2,
        in_specs=[smem] + [vmem] * 5,
        out_specs=(vmem, vmem),
        cost_estimate=pl.CostEstimate(flops=8 * first.size, bytes_accessed=24 * first.size, transcendentals=0),
        name="update",
    )(flags, first, second, mid, grad, other)


def combine_kernel(pick_ref, returned_ref, after_ref, out_ref):
    n_chip, n_expert, cap, depth = returned_ref.shape
    pick = pick_ref[...]
    for chip in range(n_chip):
        rows = returned_ref[chip].astype(jnp.float32)
        total = jnp.sum(rows, axis=0).astype(jnp.bfloat16)
        spread = lax.dot_general(
            pick, total, (((0,), (0,)), ((), ())), preferred_element_type=jnp.float32
        )
        out_ref[:, chip * depth : (chip + 1) * depth] = spread.astype(jnp.bfloat16)


def combine(pick, returned, after):
    n_chip, n_expert, cap, depth = returned.shape
    tok_dev = pick.shape[1]
    vmem = pl.BlockSpec(memory_space=pltpu.VMEM)
    return pl.pallas_call(
        combine_kernel,
        out_shape=jax.ShapeDtypeStruct((tok_dev, n_chip * depth), jnp.bfloat16),
        in_specs=[vmem, vmem, pl.BlockSpec(memory_space=pl.ANY)],
        out_specs=vmem,
        cost_estimate=pl.CostEstimate(
            flops=2 * returned.size * tok_dev, bytes_accessed=4 * tok_dev * n_chip * depth, transcendentals=0
        ),
        name="combine",
    )(pick, returned, after)


def forward_backward(chip_weights, rows_in, grads_in):
    n_chip = lax.axis_size(CHIPS)
    width_dev = chip_weights.shape[1] // 3
    bf16 = jnp.bfloat16
    pre_part = jnp.dot(rows_in, chip_weights[:, : 2 * width_dev], preferred_element_type=jnp.float32)
    grad_part = jnp.dot(grads_in, chip_weights[:, 2 * width_dev :], preferred_element_type=jnp.float32)
    parts = jnp.concatenate((pre_part, grad_part), axis=1).astype(bf16)
    if n_chip > 4:
        sums = exchange(parts.reshape(n_chip, -1, parts.shape[1]), CHIPS)
        sums = jnp.sum(sums.astype(jnp.float32), axis=0).astype(bf16)
        sums = lax.all_gather(sums, CHIPS, axis=0, tiled=True).astype(jnp.float32)
    else:
        copies = jnp.broadcast_to(parts[None], (n_chip,) + parts.shape)
        sums = jnp.sum(exchange(copies, CHIPS).astype(jnp.float32), axis=0)
    gate_pre = sums[:, :width_dev]
    up_pre = sums[:, width_dev : 2 * width_dev]
    hidden_grad = sums[:, 2 * width_dev :]
    sigma = jax.nn.sigmoid(gate_pre)
    active_part = gate_pre * sigma
    hidden = active_part * up_pre
    gate_grad = hidden_grad * up_pre * sigma * (1.0 + gate_pre * (1.0 - sigma))
    up_grad = hidden_grad * active_part
    acts = jnp.concatenate((gate_grad, up_grad, hidden), axis=1).astype(bf16)
    part_rows = lax.dot_general(
        acts[:, : 2 * width_dev],
        chip_weights[:, : 2 * width_dev],
        (((1,), (1,)), ((), ())),
        preferred_element_type=jnp.float32,
    ).astype(bf16)
    return acts, part_rows


def weight_grads(rows_in, grads_in, acts, own_depth):
    width_dev = acts.shape[1] // 3
    across = (((0,), (0,)), ((), ()))
    proj_grad = lax.dot_general(
        rows_in, acts[:, : 2 * width_dev], across, preferred_element_type=jnp.float32
    )
    down_grad = lax.dot_general(
        grads_in, acts[:, 2 * width_dev :], across, preferred_element_type=jnp.float32
    )
    grad = jnp.concatenate((proj_grad, down_grad), axis=1)
    low, high = grad[:own_depth], grad[own_depth:]
    core = lax.axis_index("core")
    other = lax.ppermute(
        jnp.where(core == 0, high, low).astype(jnp.bfloat16), "core", [(0, 1), (1, 0)]
    )
    return grad, other


def send_back(part_rows):
    return exchange(part_rows.reshape(lax.axis_size(ACROSS), CAP, part_rows.shape[1]), ACROSS)


def add_up(returned, dest_token):
    n_chip, depth = lax.axis_size(CHIPS), returned.shape[-1]
    returned = returned.reshape(n_chip, -1, depth).transpose(1, 0, 2).reshape(-1, n_chip * depth)
    return lax.dot_general(
        dest_token, returned, (((0,), (0,)), ((), ())), preferred_element_type=jnp.float32
    ).astype(jnp.bfloat16)


def one_window(pair, sends, pick, weights, first_moment, second_moment):
    low, high = pair
    own_index = lax.axis_index("expert")
    active = (own_index == low) | (own_index == high)
    move = lambda block: lax.ppermute(block, "expert", [(low, high), (high, low)])
    bf16 = jnp.bfloat16
    first, second = first_moment[0], second_moment[0]
    depth = sends.shape[-1]

    block = jnp.where(active, move(weights[0]), weights[0])
    chip_weights = lax.all_gather(block, "core", axis=0, tiled=True)
    got = exchange(sends.reshape(-1, 2 * CAP, depth), ACROSS)
    moments = jnp.concatenate((first, second)).astype(bf16)
    got, moments = lax.optimization_barrier((got, moments))
    rows_in = got[:, :CAP].reshape(-1, depth)
    grads_in = got[:, CAP:].reshape(-1, depth)
    mid = move(moments)
    acts, part_rows = forward_backward(chip_weights, rows_in, grads_in)
    returned = send_back(part_rows)
    grad, other = weight_grads(rows_in, grads_in, acts, first.shape[0])
    new_first, new_second = update(
        active, lax.axis_index("core"), first, second, mid, grad, other
    )
    returned = returned.reshape(lax.axis_size(CHIPS), -1, CAP, depth)
    return combine(pick, returned, new_first), new_first[None], new_second[None]


def many_windows(tokens, cotangent, routes, gates, layout, weights, first_moment, second_moment):
    n_expert, n_chip = lax.axis_size("expert"), lax.axis_size(CHIPS)
    n_window = n_expert // HSPLIT
    own_index = lax.axis_index("expert")
    lane_ids = jnp.arange(n_expert, dtype=jnp.int32)
    placement, xor_mask, swap_on = layout[0], layout[1, 0], layout[2]
    held_slot = jnp.where(swap_on == 1, jnp.bitwise_xor(lane_ids, xor_mask), lane_ids)
    inverse = jnp.sum(
        jnp.where(placement[None, :] == lane_ids[:, None], lane_ids[None, :], 0), axis=1
    )
    slot_owner = inverse // HSPLIT
    expert_at = jnp.sum(
        jnp.where(held_slot[:, None] == lane_ids[None, :], slot_owner[None, :], 0), axis=1
    )
    active = select_lane(swap_on, lane_ids, own_index) == 1
    bf16 = jnp.bfloat16
    block = jnp.where(active, xor_rounds(weights[0], xor_mask), weights[0])
    moments = jnp.stack((first_moment[0], second_moment[0]))
    moved = xor_rounds(moments.astype(bf16), xor_mask).astype(jnp.float32)
    moments = jnp.where(active, moved, moments)

    tok_dev, top_count = routes.shape
    own_depth = weights.shape[1]
    depth = 2 * own_depth
    flat_ids = routes.reshape(-1)
    window_ids = jnp.arange(n_window, dtype=jnp.int32)
    hit_table = (flat_ids[:, None] == window_ids[None, :]).astype(jnp.int32)
    earlier = jnp.cumsum(hit_table, axis=0) - hit_table
    position = jnp.sum(earlier * hit_table, axis=1)
    kept = (flat_ids < n_window) & (position < CAP)
    slot_key = jnp.where(kept, flat_ids * CAP + position, -1)
    slot_pick = (jnp.arange(n_window * CAP, dtype=jnp.int32)[:, None] == slot_key[None, :]).astype(
        jnp.float32
    )
    assign_pick = slot_pick.reshape(n_window * CAP, tok_dev, top_count)
    slot_token = jnp.sum(assign_pick, axis=2)
    slot_gate = jnp.sum(assign_pick * gates[None], axis=(1, 2))[:, None]
    rows = jnp.dot(slot_token.astype(bf16), tokens, preferred_element_type=jnp.float32).astype(bf16)
    grads = jnp.dot(slot_token.astype(bf16), cotangent, preferred_element_type=jnp.float32)
    grads = (grads * slot_gate).astype(bf16)
    sends = jnp.stack((rows, grads)).reshape(2, n_window, CAP, n_chip, depth)
    sends = jnp.take(sends.transpose(3, 1, 0, 2, 4), expert_at, axis=1)
    dest_token = jnp.take(slot_token.reshape(n_window, CAP, tok_dev), expert_at, axis=0)
    dest_token = dest_token.reshape(n_expert * CAP, tok_dev).astype(bf16)
    got = exchange(sends.reshape(-1, 2 * CAP, depth), ACROSS)
    rows_in = got[:, :CAP].reshape(-1, depth)
    grads_in = got[:, CAP:].reshape(-1, depth)

    chip_weights = lax.all_gather(block, "core", axis=0, tiled=True)
    acts, part_rows = forward_backward(chip_weights, rows_in, grads_in)
    grad_input = add_up(send_back(part_rows), dest_token)
    grad, other = weight_grads(rows_in, grads_in, acts, own_depth)
    core = lax.axis_index("core")
    grad = jnp.where(core == 0, grad[:own_depth], grad[own_depth:]) + other.astype(jnp.float32)
    new_first = first_decay * moments[0] + (1.0 - first_decay) * grad
    new_second = second_decay * moments[1] + (1.0 - second_decay) * grad * grad
    return grad_input, new_first[None], new_second[None]


def local(tokens, cotangent, routes, gates, layout, weights, first_moment, second_moment):
    if lax.axis_size("expert") != HSPLIT:
        return many_windows(
            tokens, cotangent, routes, gates, layout, weights, first_moment, second_moment
        )
    case, sends, pick = pick_rows(layout, routes, gates, tokens, cotangent)
    branches = [functools.partial(one_window, pair) for pair in PAIRS]
    return lax.switch(case[0, 0], branches, sends, pick, weights, first_moment, second_moment)


def solution(mesh):
    n_dp, n_expert = mesh.devices.shape
    split = Mesh(mesh.devices.reshape(n_dp // 4, 2, 2, n_expert), ROWS)
    in_specs = (
        P(ROWS, None),
        P(ROWS, None),
        P(ROWS, None),
        P(ROWS, None),
        P(),
        P("expert", DP, None),
        P("expert", DP, None),
        P("expert", DP, None),
    )
    out_specs = (P(ROWS, None), P("expert", DP, None), P("expert", DP, None))
    return jax.shard_map(local, mesh=split, in_specs=in_specs, out_specs=out_specs, check_vma=False)
```

time: 82.6 us -> 68.6 us (0.83); the launches traced: 81.7 us -> 69.7 us
  blocking collectives: 13.2 us -> 2.51 us
  Pallas kernels: 0 us -> 7.76 us
  local copies, waits for them, and re-layouts: 6.11 us -> 1.61 us
  matrix products: 5.91 us -> 2.11 us
  other arithmetic: 9.77 us -> 7.06 us
  starting transfers between devices: 18.1 us -> 19.5 us
    all_gather x2 -> x1, blocking collectives: 13.2 us -> 2.51 us  [one_window(): chip_weights = lax.all_gather(block, 'core', axis=0, tiled=True)]
    pallas_call x0 -> x3, Pallas kernels: none -> 7.76 us  [the longest x1 3.14 us: update(): pl.pallas_call(update_kernel, out_shape=(jax.ShapeDtypeStruct(first.shape...]
    another operation x28 -> x0, local copies, waits for them, and re-layouts: 5.14 us -> none
    dot_general x8 -> x5, matrix products: 5.91 us -> 2.11 us  [the longest x1 1 us: forward_backward(): lax.dot_general(acts[:, :2 * width_dev], chip_weights[:, :2 * width_dev],...]
    concatenate x2 -> x3, other arithmetic: 0.03 us -> 3.65 us  [the longest x1 2.63 us: weight_grads(): grad = jnp.concatenate((proj_grad, down_grad), axis=1)]
    broadcast_in_dim x3 -> x0, other arithmetic: 3.43 us -> none  [the longest x2 3.39 us: body(): return (grad_input, new_first[None], new_second[None])]
    reduce_sum x3 -> x1, other arithmetic: 2.27 us -> 0.1 us  [forward_backward(): sums = jnp.sum(exchange(copies, CHIPS).astype(jnp.float32), axis=0)]
    another operation x3, other arithmetic: 0.54 us -> 2.33 us
  transfers between devices with their start and end apart: 5 -> 6, of which waited for: 2 -> 3; matrix products, arithmetic and copies ran while one was open for 9% -> 12% of each run, Pallas kernels for 0% -> 5%
where the time goes in v1:
time: 68.6 us; the launch traced here: 69.7 us
  waiting for transfers between devices  27.6 us (40%)
  starting transfers between devices  19.5 us (28%)
  Pallas kernels  7.76 us (11%)
  other arithmetic  7.06 us (10%)
  blocking collectives  2.51 us (4%)
  matrix products  2.11 us (3%)
  local copies, waits for them, and re-layouts  1.61 us (2%)
  between operations  1.29 us (2%)
    all_to_all x3, waiting for transfers between devices, exchange(): return lax.all_to_all(block, axes, split_axis=0, concat_axis=0, tiled=True)  27.5 us
    all_to_all x3, starting transfers between devices, exchange(): return lax.all_to_all(block, axes, split_axis=0, concat_axis=0, tiled=True)  17.1 us
    pallas_call x1, Pallas kernels, update(): pl.pallas_call(update_kernel, out_shape=(jax.ShapeDtypeStruct(first.shape...  3.14 us
    concatenate x1, other arithmetic, weight_grads(): grad = jnp.concatenate((proj_grad, down_grad), axis=1)  2.63 us
    pallas_call x1, Pallas kernels, pick_rows(): pl.pallas_call(pick_kernel, out_shape=(jax.ShapeDtypeStruct((1, 1), jnp.i...  2.51 us
    all_gather x1, blocking collectives, one_window(): chip_weights = lax.all_gather(block, 'core', axis=0, tiled=True)  2.51 us
    ppermute x2, starting transfers between devices, one_window(): lax.ppermute(block, 'expert', [(low, high), (high, low)])  2.35 us
    pallas_call x1, Pallas kernels, combine(): pl.pallas_call(combine_kernel, out_shape=jax.ShapeDtypeStruct((tok_dev, n...  2.1 us
  transfers between devices with their start and end apart: 6, of which 3 were waited for; matrix products, arithmetic and copies ran while one was open for 12% of the time, Pallas kernels for 5%

profile of v1, /device:TPU:0, one launch (start us, length us, event | category | flops | bytes accessed | tf_op | source)
XLA Modules:
  0.0 69.7 jit_solution(2271249037267302306)
XLA Ops:
  0.6 2.5 %pick_rows.1 = (s32[1,1]{1,0:T(1,128)}, bf16[4,4,16,640]{3,2,1,0:T(8,128)(2,1)}, bf16[8,128]{1,0:T(8,128)(2,1)S(1)}) custom-call(s32[3,4]{1,0:T(4,128)} %layout_ref.1, s32[6,128]{1,0:T(8,128)} %bitcast.177, f32[6,128]{1,0:T(8,128)} %bitcast.178, bf16[128,2560]{1,0:T(8,128)(2,1)} %tokens_ref.1, bf16[128,2560]{1,0:T(8,128)(2,1)} %cot_ref.1), custom_call_target="tpu_custom_call" | custom-call | flops 10485760 | bytes 2621440 | tf_op jit(solution)/shard_map/pick_rows/pallas_call | solution.py:73
  3.8 65.9 %conditional.1 = (bf16[128,2560]{1,0:T(8,128)(2,1)}, f32[1,320,768]{2,1,0:T(8,128)}, f32[1,320,768]{2,1,0:T(8,128)}) conditional(s32[]{:T(128)} %bitcast.74, (bf16[4,4,16,640]{3,2,1,0:T(8,128)(2,1)}, f32[1,320,768]{2,1,0:T(8,128)}, f32[1,320,768]{2,1,0:T(8,128)}, bf16[1,320,768]{2,1,0:T(8,128)(2,1)}, ...), branch_computations={%region_0.2_spmd, %region_2.4_spmd, %region_4.6_spmd, %region_6.8_... | conditional | flops 366297088 | bytes 58425856 | solution.py:302
  4.0 0.7 collective-permute-start.12
  4.7 10.1 %all-to-all-start.12 = ((bf16[16,16,640]{2,1,0:T(8,128)(2,1)}), bf16[16,16,640]{2,1,0:T(8,128)(2,1)S(1)}, u32[]{:S(2)}, u32[]{:S(2)}) async-start(bf16[16,16,640]{2,1,0:T(8,128)(2,1)} %bitcast.48), calls=%async_computation.12 | async-start | bytes 655360 | tf_op jit(solution)/shard_map/cond/branch_4_fun/all_to_all | solution.py:40
  14.8 0.0 copy-start.22
  14.9 1.7 %bitcast_convert_fusion.8 = (bf16[320,768]{1,0:T(8,128)(2,1)S(1)}, bf16[320,768]{1,0:T(8,128)(2,1)S(1)}) fusion(f32[1,320,768]{2,1,0:T(8,128)} %get-tuple-element.99, f32[1,320,768]{2,1,0:T(8,128)} %get-tuple-element.98), kind=kLoop, calls=%fused_computation.207 | loop fusion | flops 491520 | bytes 2949120 | tf_op jit(solution)/shard_map/convert.39
  16.5 1.0 %pad_maximum_fusion.25 = bf16[640,768]{1,0:T(8,128)(2,1)} fusion(bf16[320,768]{1,0:T(8,128)(2,1)S(1)} %get-tuple-element.144, bf16[320,768]{1,0:T(8,128)(2,1)S(1)} %get-tuple-element.145), kind=kLoop, calls=%fused_computation.182 | loop fusion | flops 1966080 | bytes 1966080 | tf_op jit(solution)/shard_map/cond/branch_4_fun/concatenate | solution.py:221
  17.5 0.0 collective-permute-done.12
  17.5 0.0 copy-done.22
  17.5 0.1 broadcast_select_fusion.4
  17.6 2.5 %all_gather.16 = bf16[640,768]{1,0:T(8,128)(2,1)S(1)} all-gather(bf16[320,768]{1,0:T(8,128)(2,1)S(1)} %broadcast_select_fusion.4), channel_id=1, replica_groups=mesh['outer'=2,'inner'=2,'core'=2,'expert'=4] {'core'}, dimensions={0}, use_global_device_ids=true | all-gather | bytes 1474560 | tf_op jit(solution)/shard_map/cond/branch_4_fun/all_gather | solution.py:219
  20.1 11.2 %all-to-all-done.12 = bf16[16,16,640]{2,1,0:T(8,128)(2,1)S(1)} async-done(((bf16[16,16,640]{2,1,0:T(8,128)(2,1)}), bf16[16,16,640]{2,1,0:T(8,128)(2,1)S(1)}, u32[]{:S(2)}, u32[]{:S(2)}) %all-to-all-start.12) | async-done | bytes 327712 | tf_op jit(solution)/shard_map/cond/branch_4_fun/all_to_all | solution.py:40
  31.4 0.2 convolution_convert_fusion.14
  31.6 0.3 convolution_convert_fusion.13
  31.9 0.9 %broadcast_in_dim.60 = bf16[4,128,768]{2,1,0:T(8,128)(2,1)} broadcast(bf16[128,768]{1,0:T(8,128)(2,1)S(1)} %pad_maximum_fusion.26), dimensions={1,2} | broadcast | bytes 983040 | tf_op jit(solution)/shard_map/cond/branch_4_fun/broadcast_in_dim | solution.py:159
  32.8 3.5 %all-to-all-start.13 = ((bf16[4,128,768]{2,1,0:T(8,128)(2,1)}), bf16[4,128,768]{2,1,0:T(8,128)(2,1)S(1)}, u32[]{:S(2)}, u32[]{:S(2)}) async-start(bf16[4,128,768]{2,1,0:T(8,128)(2,1)} %broadcast_in_dim.60), calls=%async_computation.13 | async-start | bytes 1572864 | tf_op jit(solution)/shard_map/cond/branch_4_fun/all_to_all | solution.py:40
  36.3 1.7 %collective-permute-start.13 = (bf16[640,768]{1,0:T(8,128)(2,1)}, bf16[640,768]{1,0:T(8,128)(2,1)}, u32[]{:S(2)}, u32[]{:S(2)}) collective-permute-start(bf16[640,768]{1,0:T(8,128)(2,1)} %pad_maximum_fusion.25), channel_id=1, source_target_pairs={{1,3},{3,1},{5,7},{7,5},{9,11},{11,9},{13,15},{15,13},{17,19},{19,... | collective-permute-start | bytes 2949128 | tf_op jit(solution)/shard_map/cond/branch_4_fun/ppermute | solution.py:213
  38.0 9.6 %all-to-all-done.13 = bf16[4,128,768]{2,1,0:T(8,128)(2,1)S(1)} async-done(((bf16[4,128,768]{2,1,0:T(8,128)(2,1)}), bf16[4,128,768]{2,1,0:T(8,128)(2,1)S(1)}, u32[]{:S(2)}, u32[]{:S(2)}) %all-to-all-start.13) | async-done | bytes 786464 | tf_op jit(solution)/shard_map/cond/branch_4_fun/all_to_all | solution.py:40
  47.6 0.1 convert_reduce_fusion.4
  47.7 0.3 fusion.100
  47.9 0.0 copy-start.28
  48.0 0.1 multiply_convert_fusion.18
  48.0 0.4 fusion.103
  48.4 0.9 %fusion.95 = bf16[320,768]{1,0:T(8,128)(2,1)} fusion(f32[640,512]{1,0:T(8,128)S(1)} %fusion.103, f32[640,256]{1,0:T(8,128)S(1)} %fusion.100, pred[]{:T(512)S(6)} %eq.50), kind=kLoop, calls=%fused_computation.180 | loop fusion | flops 2211840 | bytes 2457601 | tf_op jit(solution)/shard_map/cond/branch_4_fun/convert_element_type | solution.py:192
  49.3 0.0 copy-done.28
  49.3 0.0 collective-permute-start.14
  49.3 1.0 %fusion.92 = bf16[16,8,640]{2,1,0:T(8,128)(2,1)} fusion(bf16[640,768]{1,0:T(8,128)(2,1)S(1)} %all_gather.16, bf16[128,256]{1,0:T(8,128)(2,1)S(1)} %get-tuple-element.143, bf16[128,256]{1,0:T(8,128)(2,1)S(1)} %get-tuple-element.142), kind=kOutput, calls=%fused_computation.176 | convolution fusion | flops 84230144 | bytes 950272 | tf_op jit(solution)/shard_map/cond/branch_4_fun/dot_general | solution.py:170
  50.3 3.5 %all-to-all-start.14 = ((bf16[16,8,640]{2,1,0:T(8,128)(2,1)}), bf16[16,8,640]{2,1,0:T(8,128)(2,1)S(1)}, u32[]{:S(2)}, u32[]{:S(2)}) async-start(bf16[16,8,640]{2,1,0:T(8,128)(2,1)} %fusion.92), calls=%async_computation.14 | async-start | bytes 327680 | tf_op jit(solution)/shard_map/cond/branch_4_fun/all_to_all | solution.py:40
  53.8 0.6 pad_add_fusion.4.flags_ref
  54.4 0.0 copy-start.4
  54.4 0.0 copy-start.10
  54.4 2.6 %pad_maximum_fusion.24.grad_ref = f32[640,768]{1,0:T(8,128)} fusion(f32[640,256]{1,0:T(8,128)} %copy-done.28, f32[640,512]{1,0:T(8,128)S(1)} %fusion.103), kind=kLoop, calls=%fused_computation.170 | loop fusion | flops 491520 | bytes 3932160 | tf_op jit(solution)/shard_map/cond/branch_4_fun/concatenate | solution.py:188
  57.1 0.0 collective-permute-done.13.moved_ref
  57.1 0.0 collective-permute-done.14.other_ref
  57.1 0.0 copy-done.4
  57.1 0.0 copy-done.10
  57.1 3.1 %update.10 = (f32[320,768]{1,0:T(8,128)S(1)}, f32[320,768]{1,0:T(8,128)}) custom-call(s32[2]{0:T(128)} %pad_add_fusion.4.flags_ref, f32[320,768]{1,0:T(8,128)S(1)} %bitcast.151, f32[320,768]{1,0:T(8,128)S(1)} %bitcast.157, bf16[640,768]{1,0:T(8,128)(2,1)} %collective-permute-done.13.moved_ref, f32[640,768]{1,0:T(8,128)} %pad_maximum_fusion.24.grad_ref, ...), custom_call_target="tpu_custom_call" | custom-call | flops 1966080 | bytes 5898240 | tf_op jit(solution)/shard_map/cond/branch_4_fun/update/pallas_call | solution.py:109
  60.2 0.0 copy-start.16
  60.2 6.7 %all-to-all-done.14 = bf16[16,8,640]{2,1,0:T(8,128)(2,1)S(1)} async-done(((bf16[16,8,640]{2,1,0:T(8,128)(2,1)}), bf16[16,8,640]{2,1,0:T(8,128)(2,1)S(1)}, u32[]{:S(2)}, u32[]{:S(2)}) %all-to-all-start.14) | async-done | bytes 163872 | tf_op jit(solution)/shard_map/cond/branch_4_fun/all_to_all | solution.py:40
  67.0 0.0 copy-start.34
  67.0 0.7 copy-done.34
  67.6 2.1 %combine.10 = bf16[128,2560]{1,0:T(8,128)(2,1)} custom-call(bf16[8,128]{1,0:T(8,128)(2,1)S(1)} %get-tuple-element.96.pick_ref, bf16[4,4,8,640]{3,2,1,0:T(8,128)(2,1)} %bitcast.175, f32[320,768]{1,0:T(8,128)S(1)} %get-tuple-element.103.after_ref), custom_call_target="tpu_custom_call" | custom-call | flops 20971520 | bytes 1310720 | tf_op jit(solution)/shard_map/cond/branch_4_fun/combine/pallas_call | solution.py:135
  69.7 0.0 copy-done.16
  (1 shorter events, 0.0 us)
Async XLA Ops:
  4.0 13.5 %collective-permute-start.12 = (bf16[320,768]{1,0:T(8,128)(2,1)}, bf16[320,768]{1,0:T(8,128)(2,1)S(1)}, u32[]{:S(2)}, u32[]{:S(2)}) collective-permute-start(bf16[320,768]{1,0:T(8,128)(2,1)} %bitcast.169), channel_id=1, source_target_pairs={{1,3},{3,1},{5,7},{7,5},{9,11},{11,9},{13,15},{15,13},{17,19},{19,... | collective-permute-start | bytes 1474568 | tf_op jit(solution)/shard_map/cond/branch_4_fun/ppermute | solution.py:213
  4.7 26.6 %all-to-all-start.12 = ((bf16[16,16,640]{2,1,0:T(8,128)(2,1)}), bf16[16,16,640]{2,1,0:T(8,128)(2,1)S(1)}, u32[]{:S(2)}, u32[]{:S(2)}) async-start(bf16[16,16,640]{2,1,0:T(8,128)(2,1)} %bitcast.48), calls=%async_computation.12 | async-start | bytes 655360 | tf_op jit(solution)/shard_map/cond/branch_4_fun/all_to_all | solution.py:40
  14.8 2.7 %copy-start.22 = (bf16[1,320,768]{2,1,0:T(8,128)(2,1)S(1)}, bf16[1,320,768]{2,1,0:T(8,128)(2,1)}, u32[]{:S(2)}) copy-start(bf16[1,320,768]{2,1,0:T(8,128)(2,1)} %get-tuple-element.101) | copy-start | bytes 1474564 | tf_op jit(solution)/shard_map/cond
  32.8 14.8 %all-to-all-start.13 = ((bf16[4,128,768]{2,1,0:T(8,128)(2,1)}), bf16[4,128,768]{2,1,0:T(8,128)(2,1)S(1)}, u32[]{:S(2)}, u32[]{:S(2)}) async-start(bf16[4,128,768]{2,1,0:T(8,128)(2,1)} %broadcast_in_dim.60), calls=%async_computation.13 | async-start | bytes 1572864 | tf_op jit(solution)/shard_map/cond/branch_4_fun/all_to_all | solution.py:40
  36.3 20.8 %collective-permute-start.13 = (bf16[640,768]{1,0:T(8,128)(2,1)}, bf16[640,768]{1,0:T(8,128)(2,1)}, u32[]{:S(2)}, u32[]{:S(2)}) collective-permute-start(bf16[640,768]{1,0:T(8,128)(2,1)} %pad_maximum_fusion.25), channel_id=1, source_target_pairs={{1,3},{3,1},{5,7},{7,5},{9,11},{11,9},{13,15},{15,13},{17,19},{19,... | collective-permute-start | bytes 2949128 | tf_op jit(solution)/shard_map/cond/branch_4_fun/ppermute | solution.py:213
  47.9 1.3 %copy-start.28 = (f32[640,256]{1,0:T(8,128)}, f32[640,256]{1,0:T(8,128)S(1)}, u32[]{:S(2)}) copy-start(f32[640,256]{1,0:T(8,128)S(1)} %fusion.100) | copy-start | bytes 1966084 | tf_op jit(solution)/shard_map/cond
  49.3 7.8 %collective-permute-start.14 = (bf16[320,768]{1,0:T(8,128)(2,1)}, bf16[320,768]{1,0:T(8,128)(2,1)}, u32[]{:S(2)}, u32[]{:S(2)}) collective-permute-start(bf16[320,768]{1,0:T(8,128)(2,1)} %fusion.95), channel_id=1, source_target_pairs={{0,4},{4,0},{1,5},{5,1},{2,6},{6,2},{3,7},{7,3},{8,12},{12,8},{9,1... | collective-permute-start | bytes 1474568 | tf_op jit(solution)/shard_map/cond/branch_4_fun/ppermute | solution.py:191
  50.3 16.7 %all-to-all-start.14 = ((bf16[16,8,640]{2,1,0:T(8,128)(2,1)}), bf16[16,8,640]{2,1,0:T(8,128)(2,1)S(1)}, u32[]{:S(2)}, u32[]{:S(2)}) async-start(bf16[16,8,640]{2,1,0:T(8,128)(2,1)} %fusion.92), calls=%async_computation.14 | async-start | bytes 327680 | tf_op jit(solution)/shard_map/cond/branch_4_fun/all_to_all | solution.py:40
  54.4 2.6 %copy-start.4 = (f32[1,320,768]{2,1,0:T(8,128)S(1)}, f32[1,320,768]{2,1,0:T(8,128)}, u32[]{:S(2)}) copy-start(f32[1,320,768]{2,1,0:T(8,128)} %get-tuple-element.98) | copy-start | bytes 2949124 | tf_op jit(solution)/shard_map/cond
  54.4 2.6 %copy-start.10 = (f32[1,320,768]{2,1,0:T(8,128)S(1)}, f32[1,320,768]{2,1,0:T(8,128)}, u32[]{:S(2)}) copy-start(f32[1,320,768]{2,1,0:T(8,128)} %get-tuple-element.99) | copy-start | bytes 2949124 | tf_op jit(solution)/shard_map/cond
  60.2 9.5 %copy-start.16 = (f32[320,768]{1,0:T(8,128)}, f32[320,768]{1,0:T(8,128)S(1)}, u32[]{:S(2)}) copy-start(f32[320,768]{1,0:T(8,128)S(1)} %get-tuple-element.103.after_ref) | copy-start | bytes 2949124 | tf_op jit(solution)/shard_map/cond
  67.0 0.7 copy-start.34
